TPU v7x, 512 devices: a whole 4x4x16 slice. The times are simulated.
512 devices in a mesh: row: 16 (over z), col: 8 (over x, core), layer: 4 (over y).
Axes of the slice: x: 4, y: 4, z: 16, core: 2. Of those that a mesh axis runs over, the one named last changes fastest.
Arguments:
- a_blocks: bfloat16 [8192, 16384], P('col', ('layer', 'row')), may hold values from -6 to 6
- a_mask: int32 [128, 256], P('col', ('layer', 'row')), may hold values from 0 to 1, as said below
- b_blocks: bfloat16 [16384, 8192], P(('layer', 'col'), 'row'), may hold values from -0.0625 to 0.0625
- b_mask: int32 [256, 128], P(('layer', 'col'), 'row'), may hold values 0 or 1
- c_mask: int32 [128, 128], P('col', 'row'), may hold values 0 or 1
Outputs:
- product: float32 [8192, 8192], P(('col', 'layer'), 'row')
Inputs may be any that keep to these rules, and one draw needn't show every extreme that they name: `a_mask`: 0 or 1; each row of blocks has its own share of occupied blocks.
All inputs are finite; a program needn't handle non-finite values. No bound on the sum of `b_mask` or of `c_mask` on one device may be relied on, other than what follows from the above.
Results may differ from a plain program's by a relative error of at most 0.0003.
Values may be sent and summed in bfloat16 or wider, within the bound.
A program may use at most 64 MiB of HBM per device.

v0:
```python
import jax
import jax.numpy as jnp
from jax import lax
from jax.sharding import PartitionSpec as P

BLK = 64


def expand_mask(mask, dtype):
    return jnp.repeat(jnp.repeat(mask, BLK, axis=0), BLK, axis=1).astype(dtype)


def shards(a_blocks, a_mask, b_blocks, b_mask, c_mask):
    masked_a = a_blocks * expand_mask(a_mask, jnp.bfloat16)
    masked_b = b_blocks * expand_mask(b_mask, jnp.bfloat16)
    slab_rows = lax.all_gather(masked_b, "col", axis=0, tiled=True)
    partial_value = jnp.dot(
        lax.all_gather(masked_a, "row", axis=1, tiled=True),
        slab_rows,
        preferred_element_type=jnp.float32,
    )
    partial_value = partial_value * expand_mask(c_mask, jnp.float32)
    summed = lax.psum(partial_value, "layer")
    share = summed.shape[0] // lax.axis_size("layer")
    return lax.dynamic_slice_in_dim(summed, lax.axis_index("layer") * share, share, 0)


def solution(mesh):
    in_specs = (
        P("col", ("layer", "row")),
        P("col", ("layer", "row")),
        P(("layer", "col"), "row"),
        P(("layer", "col"), "row"),
        P("col", "row"),
    )
    out_specs = P(("col", "layer"), "row")
    return jax.shard_map(shards, mesh=mesh, in_specs=in_specs, out_specs=out_specs, check_vma=False)
```

profile of v0, /device:TPU:1, one launch (start us, length us, event | category | flops | bytes accessed | tf_op | source)
XLA Modules:
  0.0 254.7 jit_solution(2217034151409825805)
XLA Ops:
  6.5 0.0 copy-start
  6.5 0.0 all-gather.5.cloned.1.call-start
  6.5 1.3 copy.10
  7.8 0.7 convert_element_type.36
  8.5 0.1 copy.9
  8.6 0.1 broadcast_in_dim.20
  8.7 0.1 convert_element_type.37
  8.8 0.8 bitcast_multiply_fusion
  9.6 0.0 all-gather.5.cloned.1.call-update
  9.6 0.0 all-gather.3.cloned.1.call-start
  9.7 1.2 copy.8
  10.9 0.7 convert_element_type.33
  11.6 0.1 broadcast_in_dim.18
  11.7 0.1 convert_element_type.34
  11.8 0.8 bitcast_multiply_fusion.1
  12.6 0.0 all-gather.3.cloned.1.call-update
  12.7 0.0 all-reduce.2.cloned.1.call-start
  12.7 0.0 copy-done
  12.7 0.1 broadcast_in_dim.22
  12.8 0.1 convert_element_type.40
  12.9 0.2 broadcast_in_dim.23
  13.1 1.8 copy.11
  15.0 40.3 %all-gather.5.cloned.1.call-done = bf16[4096,512]{0,1:T(8,128)(2,1)} async-done(((bf16[512,512]{0,1:T(8,128)(2,1)}), bf16[4096,512]{0,1:T(8,128)(2,1)}) %all-gather.5.cloned.1.call-update) | async-done | bytes 4194320 | tf_op jit(solution)/shard_map/all_gather | solution.py:16
  55.3 107.7 %all-gather.3.cloned.1.call-done = bf16[1024,4096]{0,1:T(8,128)(2,1)} async-done(((bf16[1024,256]{0,1:T(8,128)(2,1)}), bf16[1024,4096]{0,1:T(8,128)(2,1)}) %all-gather.3.cloned.1.call-update) | async-done | bytes 8388624 | tf_op jit(solution)/shard_map/all_gather | solution.py:18
  163.0 11.1 %convolution_multiply_fusion = f32[1024,512]{1,0:T(8,128)} fusion(f32[1024,512]{1,0:T(8,128)} %copy.11, bf16[1024,4096]{0,1:T(8,128)(2,1)} %all-gather.3.cloned.1.call-done, bf16[4096,512]{0,1:T(8,128)(2,1)} %all-gather.5.cloned.1.call-done), kind=kOutput, calls=%fused_computation | convolution fusion | flops 4295491584 | bytes 16777216 | tf_op jit(solution)/shard_map/dot_general | solution.py:17
  174.1 0.0 all-reduce.2.cloned.1.call-update
  174.1 72.2 %all-reduce.2.cloned.1.call-done = f32[1024,512]{1,0:T(8,128)} async-done(((f32[1024,512]{1,0:T(8,128)}), f32[1024,512]{1,0:T(8,128)}) %all-reduce.2.cloned.1.call-update) | async-done | bytes 2097168 | tf_op jit(solution)/shard_map/psum | solution.py:23
  246.3 1.9 constant_dynamic-slice_fusion
  (1 shorter events, 0.0 us)
Async XLA Ops:
  6.5 6.2 %copy-start = (s32[16,8]{0,1:T(8,128)S(1)}, s32[16,8]{0,1:T(8,128)}, u32[]{:S(2)}) copy-start(s32[16,8]{0,1:T(8,128)} %param.9) | copy-start | bytes 1540
  6.5 48.7 %all-gather.5.cloned.1.call-start = ((), (), s32[]{:S(2)}) async-start(), calls=%async_computation.1 | async-start | bytes 4718592 | tf_op jit(solution)/shard_map/all_gather | solution.py:16
  9.6 153.3 %all-gather.3.cloned.1.call-start = ((), (), s32[]{:S(2)}) async-start(), calls=%async_computation | async-start | bytes 8912896 | tf_op jit(solution)/shard_map/all_gather | solution.py:18
  12.7 233.7 %all-reduce.2.cloned.1.call-start = ((), (), s32[]{:S(2)}) async-start(), calls=%async_computation.2 | async-start | bytes 4194304 | tf_op jit(solution)/shard_map/psum | solution.py:23
Sparse Core Ops, SparseCore 0:
  9.8 45.4 all-gather.4
  57.3 105.5 all-gather.2
  174.2 72.0 all-reduce.1
where the time goes:
time: 255 us
  waiting for transfers between devices  220 us (86%)
  between operations  13.1 us (5%)
  matrix products  11.1 us (4%)
  local copies, waits for them, and re-layouts  7.05 us (3%)
  other arithmetic  3.07 us (1%)
    all_gather x1, waiting for transfers between devices, shards(): lax.all_gather(masked_a, 'row', axis=1, tiled=True)  108 us
    psum x1, waiting for transfers between devices, shards(): summed = lax.psum(partial_value, 'layer')  72.2 us
    all_gather x1, waiting for transfers between devices, shards(): slab_rows = lax.all_gather(masked_b, 'col', axis=0, tiled=True)  40.3 us
    dot_general x1, matrix products, shards(): jnp.dot(lax.all_gather(masked_a, 'row', axis=1, tiled=True), slab_rows, p...  11.1 us
  transfers between devices with their start and end apart: 3, of which 3 were waited for; matrix products, arithmetic and copies ran while one was open for 2% of the time, Pallas kernels for 0%

commit v1 on v0

v1 whole, which is shorter than its diff:
```python
import functools

import jax
import jax.numpy as jnp
from jax import lax
from jax.experimental import pallas as pl
from jax.experimental.pallas import tpu as pltpu
from jax.sharding import PartitionSpec as P

BLK = 64
MESH = pl.DeviceIdType.MESH
ORDER = (1, 3, 2, 0)


def wrap(value, size):
    return lax.rem(value + size, size)


def kernel(
    nz, nx, ny,
    a_mask, b_mask, c_mask, a_ref, b_ref, out_ref,
    am, g, bf, acc, got,
    a_send, a_recv, b_send, b_recv, c_send, c_recv,
):
    z, col, y = lax.axis_index("row"), lax.axis_index("col"), lax.axis_index("layer")
    x, core = col // 2, lax.rem(col, 2)
    half = nz // 2
    rows, depth = a_ref.shape
    grp = rows // ny
    sub = grp // 2
    bdepth, ncols = b_ref.shape

    zs = (wrap(z + 1, nz), wrap(z - 1, nz))
    xs = (wrap(x + 1, nx) * 2 + core, wrap(x - 1, nx) * 2 + core)
    sib = x * 2 + 1 - core
    opp = wrap(x + 2, nx) * 2 + core

    barrier = pltpu.get_barrier_semaphore()
    for peer in zs:
        pl.semaphore_signal(barrier, inc=1, device_id={"row": peer}, device_id_type=MESH)
    for peer in xs + (sib,):
        pl.semaphore_signal(barrier, inc=1, device_id={"col": peer}, device_id_type=MESH)
    for d in range(1, ny):
        pl.semaphore_signal(barrier, inc=1, device_id={"layer": wrap(y + d, ny)}, device_id_type=MESH)

    lane = lax.broadcasted_iota(jnp.int32, (1, 2 * BLK), 1)

    def pair(m0, m1):
        return jnp.where(lane < BLK, m0, m1).astype(jnp.float32)

    def group_of(q):
        d = jnp.where(q == 0, ORDER[0], jnp.where(q == 1, ORDER[1], jnp.where(q == 2, ORDER[2], 0)))
        return wrap(y + d, ny), d

    nb = grp // BLK
    def mask_a(t, _):
        q, r = t // nb, lax.rem(t, nb)
        src = group_of(q)[0] * nb + r
        at = pl.ds(pl.multiple_of(src * BLK, BLK), BLK)
        to = pl.ds(pl.multiple_of(t * BLK, BLK), BLK)
        for p in range(depth // (2 * BLK)):
            ls = slice(p * 2 * BLK, (p + 1) * 2 * BLK)
            m = pair(a_mask[src, 2 * p], a_mask[src, 2 * p + 1]).astype(am.dtype)
            am[to, ls] = a_ref[at, ls] * m
        return 0
    lax.fori_loop(0, rows // BLK, mask_a, 0)

    def mask_b(t, _):
        at = pl.ds(pl.multiple_of(t * BLK, BLK), BLK)
        to = pl.ds(pl.multiple_of(col * bdepth + t * BLK, BLK), BLK)
        for p in range(ncols // (2 * BLK)):
            ls = slice(p * 2 * BLK, (p + 1) * 2 * BLK)
            m = pair(b_mask[t, 2 * p], b_mask[t, 2 * p + 1]).astype(bf.dtype)
            bf[to, ls] = b_ref[at, ls] * m
        return 0
    lax.fori_loop(0, bdepth // BLK, mask_b, 0)

    pl.semaphore_wait(barrier, 5 + ny - 1)

    def chunk(ref, q, s):
        return ref.at[pl.ds(pl.multiple_of(q * grp + s * sub, sub), sub)]

    def hop(way, q, s, h):
        dst = chunk(g.at[way, h - 1], q, s)
        return dst, pltpu.make_async_remote_copy(
            src_ref=dst, dst_ref=dst,
            send_sem=a_send.at[way, q, s, h - 1], recv_sem=a_recv.at[way, q, s, h - 1],
            device_id={"row": zs[way]}, device_id_type=MESH,
        )

    def start_hop(way, q, s, h):
        dst = chunk(g.at[way, h - 1], q, s)
        def go(src):
            pltpu.make_async_remote_copy(
                src_ref=src, dst_ref=dst,
                send_sem=a_send.at[way, q, s, h - 1], recv_sem=a_recv.at[way, q, s, h - 1],
                device_id={"row": zs[way]}, device_id_type=MESH,
            ).start()
        @pl.when(h == 1)
        def _():
            go(chunk(am, q, s))
        @pl.when(h > 1)
        def _():
            go(chunk(g.at[way, jnp.maximum(h - 2, 0)], q, s))

    def b_rows(owner, first, count):
        return bf.at[pl.ds(pl.multiple_of(owner * bdepth + first, count), count)]

    hb = bdepth // 2
    def b_copy(n, owner, first, count, peer):
        ref = b_rows(owner, first, count)
        return pltpu.make_async_remote_copy(
            src_ref=ref, dst_ref=ref, send_sem=b_send.at[n], recv_sem=b_recv.at[n],
            device_id={"col": peer}, device_id_type=MESH,
        )

    b_out = (
        b_copy(0, col, 0, bdepth, xs[0]),
        b_copy(1, col, 0, bdepth, xs[1]),
        b_copy(2, xs[1], 0, hb, xs[0]),
        b_copy(3, xs[0], hb, hb, xs[1]),
        b_copy(4, col, 0, bdepth, sib),
        b_copy(5, xs[1], 0, bdepth, sib),
        b_copy(6, xs[0], 0, bdepth, sib),
        b_copy(7, opp, 0, bdepth, sib),
    )
    other = 1 - 2 * core
    b_in = (
        b_copy(0, xs[1], 0, bdepth, xs[0]),
        b_copy(1, xs[0], 0, bdepth, xs[1]),
        b_copy(2, opp, 0, hb, xs[0]),
        b_copy(3, opp, hb, hb, xs[1]),
        b_copy(4, sib, 0, bdepth, sib),
        b_copy(5, xs[1] + other, 0, bdepth, sib),
        b_copy(6, xs[0] + other, 0, bdepth, sib),
        b_copy(7, opp + other, 0, bdepth, sib),
    )

    def c_copy(q):
        target, d = group_of(q)
        return pltpu.make_async_remote_copy(
            src_ref=acc.at[q], dst_ref=got.at[q], send_sem=c_send.at[q], recv_sem=c_recv.at[q],
            device_id={"layer": target}, device_id_type=MESH,
        )

    def b_of(source):
        return bf[pl.ds(pl.multiple_of(source * depth, depth), depth), :]

    def dot(a, b):
        return jnp.dot(a, b, preferred_element_type=jnp.float32)

    def work(q, h):
        @pl.when(h == 0)
        def _():
            acc[q] = dot(am[pl.ds(pl.multiple_of(q * grp, grp), grp), :], b_of(z))
        @pl.when((h > 0) & (h < half))
        def _():
            at = pl.ds(pl.multiple_of(q * grp, grp), grp)
            n = jnp.maximum(h - 1, 0)
            acc[q] += dot(g[0, n, at, :], b_of(wrap(z - h, nz))) + dot(g[1, n, at, :], b_of(wrap(z + h, nz)))
        @pl.when(h == half)
        def _():
            source = b_of(wrap(z + half, nz))
            for s in range(2):
                at = pl.ds(pl.multiple_of(q * grp + s * sub, sub), sub)
                to = pl.ds(s * sub, sub)
                acc[q, to, :] += dot(g[s, half - 1, at, :], source)

    def settle(q):
        for s in range(2):
            hop(s, q, s, half)[1].wait_recv()

    def step(t, _):
        q, h = t // half, lax.rem(t, half) + 1
        for s in range(2):
            for way in range(2):
                @pl.when(h > 1)
                def _():
                    hop(way, q, s, jnp.maximum(h - 1, 1))[1].wait_recv()
                if way == s:
                    start_hop(way, q, s, h)
                else:
                    @pl.when(h < half)
                    def _():
                        start_hop(way, q, s, h)

        @pl.when(t == 0)
        def _():
            for n in (0, 1, 4):
                b_out[n].start()

        @pl.when((q == 0) & (h == 6))
        def _():
            for n in (0, 1):
                b_in[n].wait_recv()
            for n in (2, 3, 5, 6):
                b_out[n].start()

        @pl.when((q >= 1) & (h == 1))
        def _():
            settle(q - 1)

        @pl.when((q == 1) & (h == 1))
        def _():
            for n in (2, 3):
                b_in[n].wait_recv()
            b_out[7].start()
            for n in range(4, 8):
                b_in[n].wait_recv()

        @pl.when(q >= 1)
        def _():
            @pl.when((h == 1) & (q >= 2))
            def _():
                work(q - 1, half)
                c_copy(q - 1).start()
            work(q, h - 1)

        @pl.when(q == 1)
        def _():
            work(0, h - 1)
            @pl.when(h == half)
            def _():
                work(0, half)
                c_copy(0).start()
        return 0

    lax.fori_loop(0, ny * half, step, 0)
    last = ny - 1
    settle(last)
    work(last, half)
    for q in range(last):
        c_copy(q).wait_recv()
    for r in range(nb):
        at = pl.ds(r * BLK, BLK)
        for p in range(ncols // (2 * BLK)):
            ls = slice(p * 2 * BLK, (p + 1) * 2 * BLK)
            row = y * nb + r
            total = acc[last, at, ls] + got[0, at, ls] + got[1, at, ls] + got[2, at, ls]
            out_ref[at, ls] = total * pair(c_mask[row, 2 * p], c_mask[row, 2 * p + 1])

    def sent(t, _):
        q, h = t // half, lax.rem(t, half) + 1
        for s in range(2):
            for way in range(2):
                if way == s:
                    hop(way, q, s, h)[1].wait_send()
                else:
                    @pl.when(h < half)
                    def _():
                        hop(way, q, s, h)[1].wait_send()
        return 0
    lax.fori_loop(0, ny * half, sent, 0)
    for copy in b_out:
        copy.wait_send()
    for q in range(last):
        c_copy(q).wait_send()


def shards(nz, nx, ny, a_blocks, a_mask, b_blocks, b_mask, c_mask):
    rows, depth = a_blocks.shape
    bdepth, ncols = b_blocks.shape
    grp = rows // ny
    half = nz // 2
    vmem, smem = pl.BlockSpec(memory_space=pltpu.VMEM), pl.BlockSpec(memory_space=pltpu.SMEM)
    dma = pltpu.SemaphoreType.DMA
    return pl.pallas_call(
        functools.partial(kernel, nz, nx, ny),
        out_shape=jax.ShapeDtypeStruct((grp, ncols), jnp.float32),
        in_specs=[smem, smem, smem, vmem, vmem],
        out_specs=vmem,
        scratch_shapes=[
            pltpu.VMEM((rows, depth), jnp.bfloat16),
            pltpu.VMEM((2, half, rows, depth), jnp.bfloat16),
            pltpu.VMEM((2 * nx * bdepth, ncols), jnp.bfloat16),
            pltpu.VMEM((ny, grp, ncols), jnp.float32),
            pltpu.VMEM((ny - 1, grp, ncols), jnp.float32),
            dma((2, ny, 2, half)),
            dma((2, ny, 2, half)),
            dma((8,)),
            dma((8,)),
            dma((ny - 1,)),
            dma((ny - 1,)),
        ],
        compiler_params=pltpu.CompilerParams(
            collective_id=0, has_side_effects=True, vmem_limit_bytes=40 * 2**20
        ),
    )(a_mask, b_mask, c_mask, a_blocks, b_blocks)


def solution(mesh):
    nz, ncol, ny = mesh.shape["row"], mesh.shape["col"], mesh.shape["layer"]
    in_specs = (
        P("col", ("layer", "row")),
        P("col", ("layer", "row")),
        P(("layer", "col"), "row"),
        P(("layer", "col"), "row"),
        P("col", "row"),
    )
    out_specs = P(("col", "layer"), "row")
    body = functools.partial(shards, nz, ncol // 2, ny)
    return jax.shard_map(body, mesh=mesh, in_specs=in_specs, out_specs=out_specs, check_vma=False)
```

time: 255 us -> 140 us (0.55)
  the two profiles are of different devices: /device:TPU:1 before, /device:TPU:8 now
where the time goes in v1:
time: 140 us
  Pallas kernels  135 us (96%)
  local copies, waits for them, and re-layouts  4.34 us (3%)
    pallas_call x1, Pallas kernels, shards(): pl.pallas_call(functools.partial(kernel, nz, nx, ny), out_shape=jax.Shape...  135 us
    unnamed x11, local copies, waits for them, and re-layouts  4.34 us

profile of v1, /device:TPU:8, one launch (start us, length us, event | category | flops | bytes accessed | tf_op | source)
XLA Modules:
  0.0 139.7 jit_solution(17412761096252228762)
XLA Ops:
  0.0 0.0 copy-start.3
  0.0 0.8 copy.6.a_mask
  0.8 0.0 copy-done.3
  0.8 0.0 copy-start.2
  0.8 0.1 copy.7.c_mask
  0.9 0.6 copy-done.2
  1.5 0.0 copy-start
  1.5 1.0 copy-done
  2.5 0.0 copy-start.1
  2.5 1.0 copy-done.1
  3.5 135.4 %shard_map.55 = f32[256,512]{1,0:T(8,128)S(1)} custom-call(s32[16,4]{1,0:T(8,128)S(1)} %copy.6.a_mask, s32[8,8]{1,0:T(8,128)S(1)} %copy-done.2, s32[16,8]{1,0:T(8,128)S(1)} %copy.7.c_mask, bf16[1024,256]{1,0:T(8,128)(2,1)S(1)} %copy-done, bf16[512,512]{1,0:T(8,128)(2,1)S(1)} %copy-done.1), custom_call_target="tpu_custom_call" | custom-call | tf_op jit(solution)/shard_map/pallas_call | solution.py:267
  138.9 0.8 copy.9
Async XLA Ops:
  0.0 0.8 copy-start.3
  0.8 0.7 copy-start.2
  1.5 1.0 copy-start
  2.5 1.0 copy-start.1

commit v2 on v1

--- a/solution.py
+++ b/solution.py
@@ -11,12 +11,16 @@
 MESH = pl.DeviceIdType.MESH
 ORDER = (1, 3, 2, 0)
 
+TILES = ((4, 4), (4, 4), (3, 2), (2, 3))
+NTILES = sum(map(sum, TILES))
+UPTO = tuple(sum(map(sum, TILES[: q + 1])) for q in range(4))
+
 
 def wrap(value, size):
     return lax.rem(value + size, size)
 
 
-def kernel(
+def dense_kernel(
     nz, nx, ny,
     a_mask, b_mask, c_mask, a_ref, b_ref, out_ref,
     am, g, bf, acc, got,
@@ -257,7 +261,420 @@
         c_copy(q).wait_send()
 
 
-def shards(nz, nx, ny, a_blocks, a_mask, b_blocks, b_mask, c_mask):
+def span(q, s):
+    return sum(map(sum, TILES[:q])) + sum(TILES[q][:s]), TILES[q][s]
+
+
+def compact_kernel(
+    nz, nx, ny,
+    a_mask_hbm, b_mask_hbm, c_mask_hbm, a_hbm, b_hbm, out_ref, flag_ref,
+    a_mask, b_mask, c_mask, a_ref, b_ref, a_tiles, codes_v, codes, places_v, places,
+    ring, table, bf, staged, wide, acc, far, got, flags, flag_in,
+    in_sem, t_send, t_recv, a_send, a_recv, b_send, b_recv, c_send, c_recv, f_send, f_recv,
+):
+    z, col, y = lax.axis_index("row"), lax.axis_index("col"), lax.axis_index("layer")
+    x, core = col // 2, lax.rem(col, 2)
+    half = nz // 2
+    rows, depth = a_ref.shape
+    bdepth, ncols = b_ref.shape
+    grp = rows // ny
+    nb = grp // BLK
+    nk = depth // BLK
+
+    loads = [
+        pltpu.make_async_copy(src, dst, in_sem.at[n])
+        for n, (src, dst) in enumerate(
+            ((a_mask_hbm, a_mask), (a_hbm, a_ref), (b_mask_hbm, b_mask), (b_hbm, b_ref), (c_mask_hbm, c_mask))
+        )
+    ]
+    for load in loads:
+        load.start()
+
+    zs = (wrap(z + 1, nz), wrap(z - 1, nz))
+    ys = (wrap(y + 1, ny), wrap(y - 1, ny))
+    xs = (wrap(x + 1, nx) * 2 + core, wrap(x - 1, nx) * 2 + core)
+    sib = x * 2 + 1 - core
+    opp = wrap(x + 2, nx) * 2 + core
+
+    barrier = pltpu.get_barrier_semaphore()
+    for axis, peers in (("row", zs), ("col", xs + (sib,)), ("layer", ys)):
+        for peer in peers:
+            pl.semaphore_signal(barrier, inc=1, device_id={axis: peer}, device_id_type=MESH)
+
+    lane = lax.broadcasted_iota(jnp.int32, (1, 2 * BLK), 1)
+
+    def pair(m0, m1):
+        return jnp.where(lane < BLK, m0, m1).astype(jnp.float32)
+
+    def listed(n):
+        q, i = n // nb, lax.rem(n, nb)
+        low = i < nb // 2
+        d = jnp.where(q == 0, 2, jnp.where(q == 3, 0, jnp.where(low, 1, 3)))
+        r = jnp.where(q == 1, lax.rem(i, nb // 2), jnp.where(q == 2, nb // 2 + lax.rem(i, nb // 2), i))
+        return wrap(y + d, ny) * nb + r
+
+    loads[0].wait()
+
+    def listing(t, carry):
+        run, tile, side, bad, order, shift, place = carry
+        n, k = t // nk, lax.rem(t, nk)
+        row = listed(n)
+        m = a_mask[row, k]
+        order = jnp.where(lane == run, row * (nk // 2) + k // 2, order)
+        shift = jnp.where(lane == run, lax.rem(k, 2), shift)
+        place = jnp.where(lane == t, jnp.minimum(tile, NTILES - 1), place)
+        place = jnp.where(lane == t + BLK, m * (1 + side), place)
+        run, tile, side = run + m, tile + m * side, side + m - 2 * m * side
+        q = n // nb
+        most = jnp.where(q == 0, UPTO[0], jnp.where(q == 1, UPTO[1], jnp.where(q == 2, UPTO[2], UPTO[3]))) * 2
+        bad = jnp.where(run > most, 1, bad)
+        return run, tile, side, bad, order, shift, place
+
+    nothing = jnp.zeros((1, 2 * BLK), jnp.int32)
+    _, _, _, bad, order, shift, place = lax.fori_loop(
+        0, rows // BLK * nk, listing, (0, 0, 0, 0, nothing, nothing, nothing)
+    )
+    sub8 = lax.broadcasted_iota(jnp.int32, (8, 2 * BLK), 0)
+    codes_v[...] = jnp.where(sub8 == 0, order, shift)
+    table[0] = jnp.where(sub8 == 0, place, bad)
+    to_smem = pltpu.make_async_copy(codes_v, codes, in_sem.at[5])
+    to_smem.start()
+    loads[1].wait()
+
+    def tiled(row, _):
+        for p in range(nk // 2):
+            a_tiles[row * (nk // 2) + p] = a_ref[
+                pl.ds(pl.multiple_of(row * BLK, BLK), BLK), p * 2 * BLK : (p + 1) * 2 * BLK
+            ]
+        return 0
+
+    lax.fori_loop(0, rows // BLK, tiled, 0, unroll=4)
+    to_smem.wait()
+
+    lanes = lax.broadcasted_iota(jnp.int32, (BLK, 2 * BLK), 1)
+
+    def side_by_side(left, right, stay):
+        kept = jnp.where(lanes < BLK, left, right)
+        moved = pltpu.roll(jnp.where(lanes < BLK, right, left), BLK, 1)
+        return jnp.where(stay == 1, kept, moved)
+
+    def pack(u, _):
+        left, right = (a_tiles[codes[0, 2 * u + side]] for side in range(2))
+        stay = jnp.where(lanes < BLK, 1 - codes[1, 2 * u], codes[1, 2 * u + 1])
+        ring[0, u] = side_by_side(left, right, stay)
+        return 0
+
+    lax.fori_loop(0, UPTO[0], pack, 0, unroll=4)
+
+    def slot(way, h):
+        return jnp.where((h == 0) | (h == half), h, half * way + h)
+
+    def hop(way, q, s, h):
+        first, size = span(q, s)
+        return pltpu.make_async_remote_copy(
+            src_ref=ring.at[slot(way, h - 1), pl.ds(first, size)],
+            dst_ref=ring.at[slot(way, h), pl.ds(first, size)],
+            send_sem=a_send.at[way, q, s, h - 1], recv_sem=a_recv.at[way, q, s, h - 1],
+            device_id={"row": zs[way]}, device_id_type=MESH,
+        )
+
+    def table_hop(way, h):
+        return pltpu.make_async_remote_copy(
+            src_ref=table.at[slot(way, h - 1)], dst_ref=table.at[slot(way, h)],
+            send_sem=t_send.at[way, h - 1], recv_sem=t_recv.at[way, h - 1],
+            device_id={"row": zs[way]}, device_id_type=MESH,
+        )
+
+    def b_rows(owner, first, count):
+        return bf.at[pl.ds(pl.multiple_of(owner * bdepth + first, count), count)]
+
+    hb = bdepth // 2
+
+    def b_copy(n, owner, first, count, peer):
+        ref = b_rows(owner, first, count)
+        return pltpu.make_async_remote_copy(
+            src_ref=ref, dst_ref=ref, send_sem=b_send.at[n], recv_sem=b_recv.at[n],
+            device_id={"col": peer}, device_id_type=MESH,
+        )
+
+    b_out = (
+        b_copy(0, col, 0, bdepth, xs[0]),
+        b_copy(1, col, 0, bdepth, xs[1]),
+        b_copy(2, xs[1], 0, hb, xs[0]),
+        b_copy(3, xs[0], hb, hb, xs[1]),
+        b_copy(4, col, 0, bdepth, sib),
+        b_copy(5, xs[1], 0, bdepth, sib),
+        b_copy(6, xs[0], 0, bdepth, sib),
+        b_copy(7, opp, 0, bdepth, sib),
+    )
+    other = 1 - 2 * core
+    b_in = (
+        b_copy(0, xs[1], 0, bdepth, xs[0]),
+        b_copy(1, xs[0], 0, bdepth, xs[1]),
+        b_copy(2, opp, 0, hb, xs[0]),
+        b_copy(3, opp, hb, hb, xs[1]),
+        b_copy(4, sib, 0, bdepth, sib),
+        b_copy(5, xs[1] + other, 0, bdepth, sib),
+        b_copy(6, xs[0] + other, 0, bdepth, sib),
+        b_copy(7, opp + other, 0, bdepth, sib),
+    )
+
+    def mask_b(t, _):
+        at = pl.ds(pl.multiple_of(t * BLK, BLK), BLK)
+        to = pl.ds(pl.multiple_of(col * bdepth + t * BLK, BLK), BLK)
+        for p in range(ncols // (2 * BLK)):
+            ls = slice(p * 2 * BLK, (p + 1) * 2 * BLK)
+            m = pair(b_mask[t, 2 * p], b_mask[t, 2 * p + 1]).astype(bf.dtype)
+            bf[to, ls] = b_ref[at, ls] * m
+        return 0
+
+    hg = grp // 2
+
+    def c_copy(q, way):
+        return pltpu.make_async_remote_copy(
+            src_ref=acc.at[q, pl.ds(way * hg, hg)],
+            dst_ref=far.at[way] if q == 0 else got.at[way, q - 1],
+            send_sem=c_send.at[way, q], recv_sem=c_recv.at[way, q],
+            device_id={"layer": ys[way]}, device_id_type=MESH,
+        )
+
+    rounds = (("col", xs), ("col", xs), ("col", (sib,)), ("layer", ys), ("layer", ys))
+
+    def f_copy(n, m):
+        axis, peers = rounds[n]
+        return pltpu.make_async_remote_copy(
+            src_ref=flags.at[n], dst_ref=flag_in.at[n, m], send_sem=f_send.at[n, m], recv_sem=f_recv.at[n, m],
+            device_id={axis: peers[m]}, device_id_type=MESH,
+        )
+
+    def f_take(n):
+        value = flags[n]
+        for m in range(len(rounds[n][1])):
+            f_copy(n, m).wait_recv()
+            value = jnp.maximum(value, flag_in[n, m])
+        return value
+
+    def settle(q):
+        for s in range(2):
+            hop(s, q, s, half).wait_recv()
+
+    def table_step(h):
+        for way in range(2):
+            @pl.when(h > 1)
+            def _():
+                table_hop(way, jnp.maximum(h - 1, 1)).wait_recv()
+            if way == 0:
+                table_hop(way, h).start()
+            else:
+                @pl.when(h < half)
+                def _():
+                    table_hop(way, jnp.minimum(h, half - 1)).start()
+
+    def lanes_step(q, h, phases):
+        for qi in phases:
+            @pl.when(q == qi)
+            def _():
+                for s in range(2):
+                    for way in range(2):
+                        @pl.when(h > 1)
+                        def _():
+                            hop(way, qi, s, jnp.maximum(h - 1, 1)).wait_recv()
+                        if way == s:
+                            hop(way, qi, s, h).start()
+                        else:
+                            @pl.when(h < half)
+                            def _():
+                                hop(way, qi, s, jnp.minimum(h, half - 1)).start()
+
+    def b_of(source):
+        return bf[pl.ds(pl.multiple_of(source * depth, depth), depth), :]
+
+    def work(q, w):
+        for qi in range(4):
+            @pl.when(q == qi)
+            def _():
+                size = UPTO[qi]
+                for j in range(2):
+                    staged[j, 0:size] = ring[w + half * j, 0:size]
+        for i in range(nb):
+            for j in range(2):
+                for p in range(nk // 2):
+                    here, t = w + half * j, q * (nb * nk) + i * nk + 2 * p
+                    left, right = (staged[j, places[here, t + side]] for side in range(2))
+                    at_left, at_right = places[here, t + BLK], places[here, t + 1 + BLK]
+                    stay = jnp.where(lanes < BLK, at_left, at_right - 1)
+                    keep = pair(jnp.minimum(at_left, 1), jnp.minimum(at_right, 1)).astype(wide.dtype)
+                    to = (2 * j + p) * 2 * BLK
+                    wide[i * BLK : (i + 1) * BLK, to : to + 2 * BLK] = side_by_side(left, right, stay) * keep
+        second = jnp.where(w == 0, z + half, z + w)
+        acc[q] += jnp.dot(
+            wide[:, :depth], b_of(wrap(z - w, nz)), preferred_element_type=jnp.float32
+        ) + jnp.dot(wide[:, depth:], b_of(wrap(second, nz)), preferred_element_type=jnp.float32)
+
+    def zero(t, _):
+        acc[t // 4, pl.ds(pl.multiple_of(lax.rem(t, 4) * BLK, BLK), BLK), :] = jnp.zeros((BLK, ncols), jnp.float32)
+        return 0
+
+    pl.semaphore_wait(barrier, 7)
+
+    def step(r, _):
+        xq, xh = 2 * (r // half), lax.rem(r, half) + 1
+        yq, yh = 2 * ((r + half - 1) // half) - 1, lax.rem(r + half - 1, half) + 1
+
+        @pl.when(r < half)
+        def _():
+            table_step(r + 1)
+
+        @pl.when(r < 2 * half)
+        def _():
+            lanes_step(xq, xh, (0, 2))
+
+        @pl.when(r == 0)
+        def _():
+            lax.fori_loop(UPTO[0], NTILES, pack, 0, unroll=2)
+
+        @pl.when(r > 0)
+        def _():
+            lanes_step(yq, yh, (1, 3))
+
+        @pl.when(r == 0)
+        def _():
+            for load in loads[2:]:
+                load.wait()
+            lax.fori_loop(0, bdepth // BLK, mask_b, 0)
+            for n in (0, 1, 4):
+                b_out[n].start()
+            lax.fori_loop(0, 16, zero, 0)
+
+        @pl.when(r == 3)
+        def _():
+            for n in (0, 1):
+                b_in[n].wait_recv()
+            for n in (2, 3, 5, 6):
+                b_out[n].start()
+
+        @pl.when(r == 5)
+        def _():
+            for n in (2, 3):
+                b_in[n].wait_recv()
+            b_out[7].start()
+
+        @pl.when(r == half)
+        def _():
+            for n in range(4, 8):
+                b_in[n].wait_recv()
+            settle(0)
+            table_hop(0, half).wait_recv()
+
+            def row(j, over):
+                one = table[j]
+                places_v[pl.ds(j, 1), :] = one[0:1, :]
+                return jnp.maximum(over, one)
+
+            flags[0] = lax.fori_loop(0, nz, row, jnp.zeros((8, 2 * BLK), jnp.int32))
+            down = pltpu.make_async_copy(places_v, places, in_sem.at[6])
+            down.start()
+            down.wait()
+
+        @pl.when(r == half + 1)
+        def _():
+            settle(1)
+
+        for n in range(len(rounds)):
+            @pl.when(r == half + 1 + n)
+            def _():
+                if n:
+                    flags[n] = f_take(n - 1)
+                for m in range(len(rounds[n][1])):
+                    f_copy(n, m).start()
+
+        @pl.when(r == 2 * half)
+        def _():
+            settle(2)
+
+        def items(q, first, last):
+            def one(w, _):
+                work(q, lax.rem(w, half))
+                return 0
+            lax.fori_loop(first, last, one, 0)
+
+        late = r - half - 4
+        q = jnp.where(r < half + 2, 0, jnp.where(r < half + 4, 1, 2))
+        first = jnp.where(r < half + 4, 1 + lax.rem(r, 2) * 4, 2 * late + 1)
+        last = jnp.where(r < half, first, jnp.where(r < half + 4, first + 4, jnp.where(r < 2 * half, jnp.minimum(first + 2, half), half + 1)))
+        first = jnp.where(r == 2 * half, half, first)
+        items(q, first, last)
+
+        @pl.when(r == half + 1)
+        def _():
+            for way in range(2):
+                c_copy(0, way).start()
+
+        @pl.when(r == half + 4)
+        def _():
+            c_copy(0, 0).wait_recv()
+            acc[1, 0:hg, :] += far[0]
+            for way in range(2):
+                c_copy(1, way).start()
+
+        @pl.when(r == 2 * half)
+        def _():
+            c_copy(0, 1).wait_recv()
+            acc[2, hg:, :] += far[1]
+            for way in range(2):
+                c_copy(2, way).start()
+
+        own = 2 * (r - half - 5) + 1
+        items(3, own, jnp.where(r < half + 5, own, jnp.minimum(own + 2, half)))
+        return 0
+
+    lax.fori_loop(0, 2 * half + 1, step, 0)
+    settle(3)
+    work(3, 0)
+    for q in (1, 2):
+        for way in range(2):
+            c_copy(q, way).wait_recv()
+    for r in range(nb):
+        at = pl.ds(r * BLK, BLK)
+        part, sub = r // (nb // 2), pl.ds(r % (nb // 2) * BLK, BLK)
+        for p in range(ncols // (2 * BLK)):
+            ls = slice(p * 2 * BLK, (p + 1) * 2 * BLK)
+            row = y * nb + r
+            total = acc[3, at, ls] + got[0, part, sub, ls] + got[1, part, sub, ls]
+            out_ref[at, ls] = total * pair(c_mask[row, 2 * p], c_mask[row, 2 * p + 1])
+    flag_ref[...] = f_take(len(rounds) - 1)
+
+    def sent(t, _):
+        h = t + 1
+        table_hop(0, h).wait_send()
+
+        @pl.when(h < half)
+        def _():
+            table_hop(1, jnp.minimum(h, half - 1)).wait_send()
+
+        for q in range(4):
+            for s in range(2):
+                for way in range(2):
+                    if way == s:
+                        hop(way, q, s, h).wait_send()
+                    else:
+                        @pl.when(h < half)
+                        def _():
+                            hop(way, q, s, jnp.minimum(h, half - 1)).wait_send()
+        return 0
+
+    lax.fori_loop(0, half, sent, 0)
+    for copy in b_out:
+        copy.wait_send()
+    for q in range(3):
+        for way in range(2):
+            c_copy(q, way).wait_send()
+    for n in range(len(rounds)):
+        for m in range(len(rounds[n][1])):
+            f_copy(n, m).wait_send()
+
+
+def dense(nz, nx, ny, a_blocks, a_mask, b_blocks, b_mask, c_mask):
     rows, depth = a_blocks.shape
     bdepth, ncols = b_blocks.shape
     grp = rows // ny
@@ -265,7 +682,7 @@
     vmem, smem = pl.BlockSpec(memory_space=pltpu.VMEM), pl.BlockSpec(memory_space=pltpu.SMEM)
     dma = pltpu.SemaphoreType.DMA
     return pl.pallas_call(
-        functools.partial(kernel, nz, nx, ny),
+        functools.partial(dense_kernel, nz, nx, ny),
         out_shape=jax.ShapeDtypeStruct((grp, ncols), jnp.float32),
         in_specs=[smem, smem, smem, vmem, vmem],
         out_specs=vmem,
@@ -283,9 +700,68 @@
             dma((ny - 1,)),
         ],
         compiler_params=pltpu.CompilerParams(
+            collective_id=1, has_side_effects=True, vmem_limit_bytes=40 * 2**20
+        ),
+    )(a_mask, b_mask, c_mask, a_blocks, b_blocks)
+
+
+def compact(nz, nx, ny, a_blocks, a_mask, b_blocks, b_mask, c_mask):
+    rows, depth = a_blocks.shape
+    bdepth, ncols = b_blocks.shape
+    grp = rows // ny
+    half = nz // 2
+    vmem, anywhere = pl.BlockSpec(memory_space=pltpu.VMEM), pl.BlockSpec(memory_space=pl.ANY)
+    dma = pltpu.SemaphoreType.DMA
+    return pl.pallas_call(
+        functools.partial(compact_kernel, nz, nx, ny),
+        out_shape=(
+            jax.ShapeDtypeStruct((grp, ncols), jnp.float32),
+            jax.ShapeDtypeStruct((8, 128), jnp.int32),
+        ),
+        in_specs=[anywhere] * 5,
+        out_specs=(vmem, vmem),
+        scratch_shapes=[
+            pltpu.SMEM(a_mask.shape, jnp.int32),
+            pltpu.SMEM(b_mask.shape, jnp.int32),
+            pltpu.SMEM(c_mask.shape, jnp.int32),
+            pltpu.VMEM((rows, depth), jnp.bfloat16),
+            pltpu.VMEM((bdepth, ncols), jnp.bfloat16),
+            pltpu.VMEM((rows * depth // (2 * BLK * BLK), BLK, 2 * BLK), jnp.bfloat16),
+            pltpu.VMEM((8, 128), jnp.int32),
+            pltpu.SMEM((8, 128), jnp.int32),
+            pltpu.VMEM((nz, 128), jnp.int32),
+            pltpu.SMEM((nz, 128), jnp.int32),
+            pltpu.VMEM((nz, NTILES, BLK, 2 * BLK), jnp.bfloat16),
+            pltpu.VMEM((nz, 8, 128), jnp.int32),
+            pltpu.VMEM((2 * nx * bdepth, ncols), jnp.bfloat16),
+            pltpu.VMEM((2, NTILES, BLK, 2 * BLK), jnp.bfloat16),
+            pltpu.VMEM((grp, 2 * depth), jnp.bfloat16),
+            pltpu.VMEM((ny, grp, ncols), jnp.float32),
+            pltpu.VMEM((2, grp // 2, ncols), jnp.float32),
+            pltpu.VMEM((2, 2, grp // 2, ncols), jnp.float32),
+            pltpu.VMEM((5, 8, 128), jnp.int32),
+            pltpu.VMEM((5, 2, 8, 128), jnp.int32),
+            dma((7,)),
+            dma((2, half)),
+            dma((2, half)),
+            dma((2, 4, 2, half)),
+            dma((2, 4, 2, half)),
+            dma((8,)),
+            dma((8,)),
+            dma((2, 3)),
+            dma((2, 3)),
+            dma((5, 2)),
+            dma((5, 2)),
+        ],
+        compiler_params=pltpu.CompilerParams(
             collective_id=0, has_side_effects=True, vmem_limit_bytes=40 * 2**20
         ),
     )(a_mask, b_mask, c_mask, a_blocks, b_blocks)
+
+
+def shards(nz, nx, ny, *args):
+    product, flag = compact(nz, nx, ny, *args)
+    return lax.cond(flag[1, 0] > 0, lambda: dense(nz, nx, ny, *args), lambda: product)
 
 
 def solution(mesh):

time: 140 us -> 105 us (0.75)
  the two profiles are of different devices: /device:TPU:8 before, /device:TPU:2 now
where the time goes in v2:
time: 105 us
  Pallas kernels  101 us (96%)
  local copies, waits for them, and re-layouts  2.78 us (3%)
    pallas_call x1, Pallas kernels, compact(): pl.pallas_call(functools.partial(compact_kernel, nz, nx, ny), out_shape=(...  101 us
    unnamed x13, local copies, waits for them, and re-layouts  2.27 us

profile of v2, /device:TPU:2, one launch (start us, length us, event | category | flops | bytes accessed | tf_op | source)
XLA Modules:
  0.0 104.6 jit_solution(4323004876256063641)
XLA Ops:
  0.0 0.0 copy-start.3
  0.0 0.8 copy.8.a_mask_hbm
  0.8 0.0 copy-done.3
  0.8 0.0 copy-start.2
  0.8 0.1 copy.9.c_mask_hbm
  0.9 0.6 copy-done.2
  1.5 0.0 copy-start
  1.5 0.0 copy-start.1
  1.5 101.1 %shard_map.57 = (f32[256,512]{1,0:T(8,128)S(1)}, s32[8,128]{1,0:T(8,128)S(1)}) custom-call(s32[16,4]{1,0:T(8,128)S(1)} %copy.8.a_mask_hbm, s32[8,8]{1,0:T(8,128)S(1)} %copy-done.2, s32[16,8]{1,0:T(8,128)S(1)} %copy.9.c_mask_hbm, bf16[1024,256]{1,0:T(8,128)(2,1)} %a_hbm.1, bf16[512,512]{1,0:T(8,128)(2,1)} %b_hbm.1), custom_call_target="tpu_custom_call" | custom-call | tf_op jit(solution)/shard_map/pallas_call | solution.py:715
  102.6 0.5 slice.3
  103.1 0.0 copy-start.4
  103.8 0.0 copy-done
  103.8 0.0 copy-done.1
  103.8 0.0 copy-done.4
  103.9 0.8 copy.15
  (1 shorter events, 0.0 us)
Async XLA Ops:
  0.0 0.8 copy-start.3
  0.8 0.7 copy-start.2
  1.5 102.3 %copy-start = (bf16[1024,256]{1,0:T(8,128)(2,1)S(1)}, bf16[1024,256]{1,0:T(8,128)(2,1)}, u32[]{:S(2)}) copy-start(bf16[1024,256]{1,0:T(8,128)(2,1)} %a_hbm.1) | copy-start | bytes 1572868
  1.5 102.4 %copy-start.1 = (bf16[512,512]{1,0:T(8,128)(2,1)S(1)}, bf16[512,512]{1,0:T(8,128)(2,1)}, u32[]{:S(2)}) copy-start(bf16[512,512]{1,0:T(8,128)(2,1)} %b_hbm.1) | copy-start | bytes 1572868
  103.1 0.7 copy-start.4

commit v3 on v2

--- a/solution.py
+++ b/solution.py
@@ -11,9 +11,50 @@
 MESH = pl.DeviceIdType.MESH
 ORDER = (1, 3, 2, 0)
 
-TILES = ((4, 4), (4, 4), (3, 2), (2, 3))
+TILES = ((4, 4), (4, 4), (3, 2), (3, 2))
 NTILES = sum(map(sum, TILES))
 UPTO = tuple(sum(map(sum, TILES[: q + 1])) for q in range(4))
+
+READY = 24
+
+HOPS = (
+    0, 3, 1, 0, 3, 1, 0, 2, 3, 1, 0, 2, 3, 1, 0, 2, 3, 1, 0, 4, 2, 3, 1, 0, 5, 4, 2, 3, 1, 0,
+    5, 4, 6, 2, 5, 4, 7, 6, 2, 5, 4, 7, 6, 2, 5, 4, 7, 6, 5, 4, 7, 6, 5, 4, 7, 6, 7, 6, 7, 6,
+)
+
+
+def plan(half):
+    taken, hops, settled, jobs, sends = [0] * 8, [], [], [], []
+    done, worked = set(), set()
+    last = [max(i for i, chunk in enumerate(HOPS) if chunk // 2 == q) for q in range(4)]
+    todo = [(q, w % half) for q in range(4) for w in range(1, half + 1)]
+    i = 0
+    while len(worked) < len(todo):
+        hops.append(None)
+        if i < len(HOPS):
+            chunk = HOPS[i]
+            taken[chunk] += 1
+            hops[i] = (chunk // 2, chunk % 2, taken[chunk])
+        settled.append([q for q in range(4) if q not in done and i >= min(last[q] + 2, len(HOPS) + (q == 3))])
+        done.update(settled[i])
+        arrived = [half if q in done else min(taken[2 * q], taken[2 * q + 1]) - 1 for q in range(4)]
+        job = -1
+        for q, w in todo:
+            if (
+                i >= READY
+                and (q, w) not in worked
+                and (w or half) <= arrived[q]
+                and (q == 0 or (q - 1, w) in worked)
+            ):
+                job = q * half + w
+                worked.add((q, w))
+                break
+        jobs.append(job)
+        for q in range(3):
+            if len(sends) == q and all((q, w) in worked for w in range(half)):
+                sends.append(max(i, sends[-1] + 3) if sends else i)
+        i += 1
+    return hops, settled, jobs, sends
 
 
 def wrap(value, size):
@@ -319,7 +360,7 @@
         run, tile, side, bad, order, shift, place = carry
         n, k = t // nk, lax.rem(t, nk)
         row = listed(n)
-        m = a_mask[row, k]
+        m = a_mask[k, row]
         order = jnp.where(lane == run, row * (nk // 2) + k // 2, order)
         shift = jnp.where(lane == run, lax.rem(k, 2), shift)
         place = jnp.where(lane == t, jnp.minimum(tile, NTILES - 1), place)
@@ -332,7 +373,7 @@
 
     nothing = jnp.zeros((1, 2 * BLK), jnp.int32)
     _, _, _, bad, order, shift, place = lax.fori_loop(
-        0, rows // BLK * nk, listing, (0, 0, 0, 0, nothing, nothing, nothing)
+        0, rows // BLK * nk, listing, (0, 0, 0, 0, nothing, nothing, nothing), unroll=8
     )
     sub8 = lax.broadcasted_iota(jnp.int32, (8, 2 * BLK), 0)
     codes_v[...] = jnp.where(sub8 == 0, order, shift)
@@ -367,7 +408,7 @@
     lax.fori_loop(0, UPTO[0], pack, 0, unroll=4)
 
     def slot(way, h):
-        return jnp.where((h == 0) | (h == half), h, half * way + h)
+        return h if h in (0, half) else half * way + h
 
     def hop(way, q, s, h):
         first, size = span(q, s)
@@ -457,56 +498,43 @@
     def settle(q):
         for s in range(2):
             hop(s, q, s, half).wait_recv()
+            hop(1 - s, q, s, half - 1).wait_recv()
 
     def table_step(h):
         for way in range(2):
-            @pl.when(h > 1)
-            def _():
-                table_hop(way, jnp.maximum(h - 1, 1)).wait_recv()
-            if way == 0:
+            if h > 1:
+                table_hop(way, h - 1).wait_recv()
+            if way == 0 or h < half:
                 table_hop(way, h).start()
-            else:
-                @pl.when(h < half)
-                def _():
-                    table_hop(way, jnp.minimum(h, half - 1)).start()
-
-    def lanes_step(q, h, phases):
-        for qi in phases:
-            @pl.when(q == qi)
-            def _():
-                for s in range(2):
-                    for way in range(2):
-                        @pl.when(h > 1)
-                        def _():
-                            hop(way, qi, s, jnp.maximum(h - 1, 1)).wait_recv()
-                        if way == s:
-                            hop(way, qi, s, h).start()
-                        else:
-                            @pl.when(h < half)
-                            def _():
-                                hop(way, qi, s, jnp.minimum(h, half - 1)).start()
+
+    def take_hop(q, s, h):
+        for way in range(2):
+            piece = s if way == 0 else 1 - s
+            if h > 1:
+                hop(way, q, piece, h - 1).wait_recv()
+            hop(way, q, piece, h).start()
 
     def b_of(source):
         return bf[pl.ds(pl.multiple_of(source * depth, depth), depth), :]
 
     def work(q, w):
-        for qi in range(4):
-            @pl.when(q == qi)
-            def _():
-                size = UPTO[qi]
-                for j in range(2):
-                    staged[j, 0:size] = ring[w + half * j, 0:size]
+        first, size = span(q, 0)[0], sum(TILES[q])
+        for j in range(2):
+            staged[w + half * j, first : first + size] = ring[w + half * j, first : first + size]
         for i in range(nb):
             for j in range(2):
                 for p in range(nk // 2):
                     here, t = w + half * j, q * (nb * nk) + i * nk + 2 * p
-                    left, right = (staged[j, places[here, t + side]] for side in range(2))
+                    left, right = (staged[here, places[here, t + side]] for side in range(2))
                     at_left, at_right = places[here, t + BLK], places[here, t + 1 + BLK]
-                    stay = jnp.where(lanes < BLK, at_left, at_right - 1)
-                    keep = pair(jnp.minimum(at_left, 1), jnp.minimum(at_right, 1)).astype(wide.dtype)
+                    kept = pair(jnp.where(at_left == 1, 1, 0), jnp.where(at_right == 2, 1, 0)).astype(wide.dtype)
+                    moved = pair(jnp.where(at_left == 2, 1, 0), jnp.where(at_right == 1, 1, 0)).astype(wide.dtype)
                     to = (2 * j + p) * 2 * BLK
-                    wide[i * BLK : (i + 1) * BLK, to : to + 2 * BLK] = side_by_side(left, right, stay) * keep
-        second = jnp.where(w == 0, z + half, z + w)
+                    wide[i * BLK : (i + 1) * BLK, to : to + 2 * BLK] = (
+                        jnp.where(lanes < BLK, left, right) * kept
+                        + pltpu.roll(jnp.where(lanes < BLK, right, left), BLK, 1) * moved
+                    )
+        second = z + (w or half)
         acc[q] += jnp.dot(
             wide[:, :depth], b_of(wrap(z - w, nz)), preferred_element_type=jnp.float32
         ) + jnp.dot(wide[:, depth:], b_of(wrap(second, nz)), preferred_element_type=jnp.float32)
@@ -517,53 +545,38 @@
 
     pl.semaphore_wait(barrier, 7)
 
-    def step(r, _):
-        xq, xh = 2 * (r // half), lax.rem(r, half) + 1
-        yq, yh = 2 * ((r + half - 1) // half) - 1, lax.rem(r + half - 1, half) + 1
-
-        @pl.when(r < half)
-        def _():
-            table_step(r + 1)
-
-        @pl.when(r < 2 * half)
-        def _():
-            lanes_step(xq, xh, (0, 2))
-
-        @pl.when(r == 0)
-        def _():
+    hops, settled, jobs, sends = plan(half)
+    stages = len(hops)
+
+    def at_stage(i):
+        if i < len(HOPS):
+            take_hop(*hops[i])
+        if i == 0:
             lax.fori_loop(UPTO[0], NTILES, pack, 0, unroll=2)
-
-        @pl.when(r > 0)
-        def _():
-            lanes_step(yq, yh, (1, 3))
-
-        @pl.when(r == 0)
-        def _():
+        if i == 2:
             for load in loads[2:]:
                 load.wait()
             lax.fori_loop(0, bdepth // BLK, mask_b, 0)
             for n in (0, 1, 4):
                 b_out[n].start()
+        if i == 3:
             lax.fori_loop(0, 16, zero, 0)
-
-        @pl.when(r == 3)
-        def _():
+        if i % 3 == 0 and i < 3 * half:
+            table_step(i // 3 + 1)
+        if i == 13:
             for n in (0, 1):
                 b_in[n].wait_recv()
             for n in (2, 3, 5, 6):
                 b_out[n].start()
-
-        @pl.when(r == 5)
-        def _():
+        if i == 18:
             for n in (2, 3):
                 b_in[n].wait_recv()
             b_out[7].start()
-
-        @pl.when(r == half)
-        def _():
+        for q in settled[i]:
+            settle(q)
+        if i == READY:
             for n in range(4, 8):
                 b_in[n].wait_recv()
-            settle(0)
             table_hop(0, half).wait_recv()
 
             def row(j, over):
@@ -575,62 +588,27 @@
             down = pltpu.make_async_copy(places_v, places, in_sem.at[6])
             down.start()
             down.wait()
-
-        @pl.when(r == half + 1)
-        def _():
-            settle(1)
-
-        for n in range(len(rounds)):
-            @pl.when(r == half + 1 + n)
-            def _():
-                if n:
-                    flags[n] = f_take(n - 1)
-                for m in range(len(rounds[n][1])):
-                    f_copy(n, m).start()
-
-        @pl.when(r == 2 * half)
-        def _():
-            settle(2)
-
-        def items(q, first, last):
-            def one(w, _):
-                work(q, lax.rem(w, half))
-                return 0
-            lax.fori_loop(first, last, one, 0)
-
-        late = r - half - 4
-        q = jnp.where(r < half + 2, 0, jnp.where(r < half + 4, 1, 2))
-        first = jnp.where(r < half + 4, 1 + lax.rem(r, 2) * 4, 2 * late + 1)
-        last = jnp.where(r < half, first, jnp.where(r < half + 4, first + 4, jnp.where(r < 2 * half, jnp.minimum(first + 2, half), half + 1)))
-        first = jnp.where(r == 2 * half, half, first)
-        items(q, first, last)
-
-        @pl.when(r == half + 1)
-        def _():
-            for way in range(2):
-                c_copy(0, way).start()
-
-        @pl.when(r == half + 4)
-        def _():
-            c_copy(0, 0).wait_recv()
-            acc[1, 0:hg, :] += far[0]
-            for way in range(2):
-                c_copy(1, way).start()
-
-        @pl.when(r == 2 * half)
-        def _():
-            c_copy(0, 1).wait_recv()
-            acc[2, hg:, :] += far[1]
-            for way in range(2):
-                c_copy(2, way).start()
-
-        own = 2 * (r - half - 5) + 1
-        items(3, own, jnp.where(r < half + 5, own, jnp.minimum(own + 2, half)))
-        return 0
-
-    lax.fori_loop(0, 2 * half + 1, step, 0)
-    settle(3)
-    work(3, 0)
+        n, late = divmod(i - READY - 2, 4)
+        if late == 0 and 0 <= n < len(rounds):
+            if n:
+                flags[n] = f_take(n - 1)
+            for m in range(len(rounds[n][1])):
+                f_copy(n, m).start()
+
+    def after_stage(i):
+        for q in range(3):
+            if i == sends[q]:
+                if q:
+                    c_copy(0, q - 1).wait_recv()
+                    acc[q, (q - 1) * hg : q * hg, :] += far[q - 1]
+                for way in range(2):
+                    c_copy(q, way).start()
+
+    for i in range(stages):
+        at_stage(i)
+        if jobs[i] >= 0:
+            work(jobs[i] // half, jobs[i] % half)
+        after_stage(i)
     for q in (1, 2):
         for way in range(2):
             c_copy(q, way).wait_recv()
@@ -641,29 +619,18 @@
             ls = slice(p * 2 * BLK, (p + 1) * 2 * BLK)
             row = y * nb + r
             total = acc[3, at, ls] + got[0, part, sub, ls] + got[1, part, sub, ls]
-            out_ref[at, ls] = total * pair(c_mask[row, 2 * p], c_mask[row, 2 * p + 1])
+            out_ref[at, ls] = total * pair(c_mask[2 * p, row], c_mask[2 * p + 1, row])
     flag_ref[...] = f_take(len(rounds) - 1)
 
-    def sent(t, _):
-        h = t + 1
+    for h in range(1, half + 1):
         table_hop(0, h).wait_send()
-
-        @pl.when(h < half)
-        def _():
-            table_hop(1, jnp.minimum(h, half - 1)).wait_send()
-
+        if h < half:
+            table_hop(1, h).wait_send()
         for q in range(4):
             for s in range(2):
                 for way in range(2):
-                    if way == s:
+                    if way == s or h < half:
                         hop(way, q, s, h).wait_send()
-                    else:
-                        @pl.when(h < half)
-                        def _():
-                            hop(way, q, s, jnp.minimum(h, half - 1)).wait_send()
-        return 0
-
-    lax.fori_loop(0, half, sent, 0)
     for copy in b_out:
         copy.wait_send()
     for q in range(3):
@@ -721,9 +688,9 @@
         in_specs=[anywhere] * 5,
         out_specs=(vmem, vmem),
         scratch_shapes=[
-            pltpu.SMEM(a_mask.shape, jnp.int32),
+            pltpu.SMEM(a_mask.shape[::-1], jnp.int32),
             pltpu.SMEM(b_mask.shape, jnp.int32),
-            pltpu.SMEM(c_mask.shape, jnp.int32),
+            pltpu.SMEM(c_mask.shape[::-1], jnp.int32),
             pltpu.VMEM((rows, depth), jnp.bfloat16),
             pltpu.VMEM((bdepth, ncols), jnp.bfloat16),
             pltpu.VMEM((rows * depth // (2 * BLK * BLK), BLK, 2 * BLK), jnp.bfloat16),
@@ -734,7 +701,7 @@
             pltpu.VMEM((nz, NTILES, BLK, 2 * BLK), jnp.bfloat16),
             pltpu.VMEM((nz, 8, 128), jnp.int32),
             pltpu.VMEM((2 * nx * bdepth, ncols), jnp.bfloat16),
-            pltpu.VMEM((2, NTILES, BLK, 2 * BLK), jnp.bfloat16),
+            pltpu.VMEM((nz, NTILES, BLK, 2 * BLK), jnp.bfloat16),
             pltpu.VMEM((grp, 2 * depth), jnp.bfloat16),
             pltpu.VMEM((ny, grp, ncols), jnp.float32),
             pltpu.VMEM((2, grp // 2, ncols), jnp.float32),
@@ -756,7 +723,7 @@
         compiler_params=pltpu.CompilerParams(
             collective_id=0, has_side_effects=True, vmem_limit_bytes=40 * 2**20
         ),
-    )(a_mask, b_mask, c_mask, a_blocks, b_blocks)
+    )(a_mask.T, b_mask, c_mask.T, a_blocks, b_blocks)
 
 
 def shards(nz, nx, ny, *args):

time: 105 us -> 96.8 us (0.922)
  the two profiles are of different devices: /device:TPU:2 before, /device:TPU:16 now
where the time goes in v3:
time: 96.8 us; the launch traced here: 96.6 us
  Pallas kernels  93.8 us (97%)
  local copies, waits for them, and re-layouts  2.01 us (2%)
    pallas_call x1, Pallas kernels, compact(): pl.pallas_call(functools.partial(compact_kernel, nz, nx, ny), out_shape=(...  93.8 us

profile of v3, /device:TPU:16, one launch (start us, length us, event | category | flops | bytes accessed | tf_op | source)
XLA Modules:
  0.0 96.6 jit_solution(187399529993954943)
XLA Ops:
  0.0 0.0 copy-start.2
  0.0 0.7 copy-done.2
  0.7 0.0 copy-start
  0.7 0.0 copy-start.1
  0.7 93.8 %shard_map.57 = (f32[256,512]{1,0:T(8,128)S(1)}, s32[8,128]{1,0:T(8,128)S(1)}) custom-call(s32[4,16]{1,0:T(4,128)} %bitcast.4, s32[8,8]{1,0:T(8,128)S(1)} %copy-done.2, s32[8,16]{1,0:T(8,128)} %bitcast.3, bf16[1024,256]{1,0:T(8,128)(2,1)} %a_hbm.1, bf16[512,512]{1,0:T(8,128)(2,1)} %b_hbm.1), custom_call_target="tpu_custom_call" | custom-call | tf_op jit(solution)/shard_map/pallas_call | solution.py:682
  94.5 0.0 copy-start.3
  94.6 0.5 slice.3
  95.1 0.0 copy-start.4
  95.7 0.0 copy-done
  95.8 0.0 copy-done.1
  95.8 0.0 copy-done.3
  95.8 0.0 copy-done.4
  95.8 0.8 copy.13
  (1 shorter events, 0.0 us)
Async XLA Ops:
  0.0 0.7 copy-start.2
  0.7 95.1 %copy-start = (bf16[1024,256]{1,0:T(8,128)(2,1)S(1)}, bf16[1024,256]{1,0:T(8,128)(2,1)}, u32[]{:S(2)}) copy-start(bf16[1024,256]{1,0:T(8,128)(2,1)} %a_hbm.1) | copy-start | bytes 1572868
  0.7 95.1 %copy-start.1 = (bf16[512,512]{1,0:T(8,128)(2,1)S(1)}, bf16[512,512]{1,0:T(8,128)(2,1)}, u32[]{:S(2)}) copy-start(bf16[512,512]{1,0:T(8,128)(2,1)} %b_hbm.1) | copy-start | bytes 1572868
  94.5 1.2 %copy-start.3 = (s32[16,8]{0,1:T(8,128)S(1)}, s32[16,8]{0,1:T(8,128)}, u32[]{:S(2)}) copy-start(s32[16,8]{0,1:T(8,128)} %param.11) | copy-start | bytes 1540
  95.1 0.7 copy-start.4

commit v4 on v3

--- a/solution.py
+++ b/solution.py
@@ -553,13 +553,13 @@
             take_hop(*hops[i])
         if i == 0:
             lax.fori_loop(UPTO[0], NTILES, pack, 0, unroll=2)
-        if i == 2:
+        if i == 1:
             for load in loads[2:]:
                 load.wait()
             lax.fori_loop(0, bdepth // BLK, mask_b, 0)
             for n in (0, 1, 4):
                 b_out[n].start()
-        if i == 3:
+        if i == 22:
             lax.fori_loop(0, 16, zero, 0)
         if i % 3 == 0 and i < 3 * half:
             table_step(i // 3 + 1)

time: 96.8 us -> 96.8 us (level)
  no operation moved by 1% of the time
where the time goes in v4:
time: 96.8 us; the launch traced here: 96.6 us
  Pallas kernels  93.8 us (97%)
  local copies, waits for them, and re-layouts  2.01 us (2%)
    pallas_call x1, Pallas kernels, compact(): pl.pallas_call(functools.partial(compact_kernel, nz, nx, ny), out_shape=(...  93.8 us

profile of v4, /device:TPU:16, one launch (start us, length us, event | category | flops | bytes accessed | tf_op | source)
XLA Modules:
  0.0 96.6 jit_solution(16293066902364847928)
XLA Ops:
  0.0 0.0 copy-start.2
  0.0 0.7 copy-done.2
  0.7 0.0 copy-start
  0.7 0.0 copy-start.1
  0.7 93.8 %shard_map.57 = (f32[256,512]{1,0:T(8,128)S(1)}, s32[8,128]{1,0:T(8,128)S(1)}) custom-call(s32[4,16]{1,0:T(4,128)} %bitcast.4, s32[8,8]{1,0:T(8,128)S(1)} %copy-done.2, s32[8,16]{1,0:T(8,128)} %bitcast.3, bf16[1024,256]{1,0:T(8,128)(2,1)} %a_hbm.1, bf16[512,512]{1,0:T(8,128)(2,1)} %b_hbm.1), custom_call_target="tpu_custom_call" | custom-call | tf_op jit(solution)/shard_map/pallas_call | solution.py:682
  94.5 0.0 copy-start.3
  94.6 0.5 slice.3
  95.1 0.0 copy-start.4
  95.7 0.0 copy-done
  95.8 0.0 copy-done.1
  95.8 0.0 copy-done.3
  95.8 0.0 copy-done.4
  95.8 0.8 copy.13
  (1 shorter events, 0.0 us)
Async XLA Ops:
  0.0 0.7 copy-start.2
  0.7 95.1 %copy-start = (bf16[1024,256]{1,0:T(8,128)(2,1)S(1)}, bf16[1024,256]{1,0:T(8,128)(2,1)}, u32[]{:S(2)}) copy-start(bf16[1024,256]{1,0:T(8,128)(2,1)} %a_hbm.1) | copy-start | bytes 1572868
  0.7 95.1 %copy-start.1 = (bf16[512,512]{1,0:T(8,128)(2,1)S(1)}, bf16[512,512]{1,0:T(8,128)(2,1)}, u32[]{:S(2)}) copy-start(bf16[512,512]{1,0:T(8,128)(2,1)} %b_hbm.1) | copy-start | bytes 1572868
  94.5 1.2 %copy-start.3 = (s32[16,8]{0,1:T(8,128)S(1)}, s32[16,8]{0,1:T(8,128)}, u32[]{:S(2)}) copy-start(s32[16,8]{0,1:T(8,128)} %param.11) | copy-start | bytes 1540
  95.1 0.7 copy-start.4
